TPU v7x, 128 devices: a whole 4x4x4 slice. The times are simulated.
128 devices in a mesh: sec: 4 (over x), dev: 32 (over z, y, core).
Axes of the slice: x: 4, y: 4, z: 4, core: 2. Of those that a mesh axis runs over, the one named last changes fastest.
Arguments:
- strain_rows: bfloat16 [262144, 128], P(('sec', 'dev')), may hold values from -6 to 6
- bands: int32 [262144], P(('sec', 'dev')), may hold values from 0 to 15
- damaged: int32 [16384], P(('sec', 'dev')), may hold values from 0 to 2047
- owner: int32 [16384, 1], P(('sec', 'dev')), may hold values from 0 to 127; in each aligned block of 128 rows (0 to 127, 128 to 255, ...) at most 2 rows name the same one
- first_layers: bfloat16 [16384, 4096], P(('sec', 'dev')), may hold values from -0.5 to 0.5
- middle_weight: bfloat16 [4096, 4096], P(None, 'sec'), may hold values from -0.09375 to 0.09375
- out_weight: bfloat16 [4096, 128], P('sec'), may hold values from -0.09375 to 0.09375
- band_scale: float32 [16, 4096], replicated, may hold values from 0.5 to 2
- back_weight: bfloat16 [128, 128], replicated, may hold values from -0.5 to 0.5
Outputs:
- response: bfloat16 [16384, 128], P(('sec', 'dev'))
Inputs may be any that keep to these rules, and one draw needn't show every extreme that they name: Among the 128 rows of one macro device no owner is named more than 2 times, a bound that some block reaches. `damaged`: indices into the listing device's own 2048 points.
All inputs are finite; a program needn't handle non-finite values.
Results may differ from a plain program's by a relative error of at most 0.014.
Values may be sent and summed in bfloat16 or wider, within the bound.
A program may use at most 128 MiB of HBM per device.

v0:
```python
import jax
import jax.numpy as jnp
from jax import lax
from jax.sharding import PartitionSpec as P

PASSES = 2


def band_rows(band_values, band_scale):
    levels = jnp.arange(band_scale.shape[0], dtype=jnp.float32)
    picks = (band_values.astype(jnp.float32)[:, None] == levels[None, :]).astype(jnp.float32)
    return jnp.dot(
        picks, band_scale, precision=lax.Precision.HIGHEST, preferred_element_type=jnp.float32
    )


def first_hidden(row_block, weight_block, band_block, band_scale):
    mixed = jnp.dot(row_block, weight_block, preferred_element_type=jnp.float32) * band_rows(
        band_block, band_scale
    )
    return jax.nn.silu(mixed).astype(jnp.bfloat16)


def surrogate_tail(hidden_block, middle_weight, out_weight):
    middle = jax.nn.silu(
        jnp.dot(hidden_block, middle_weight, preferred_element_type=jnp.float32)
    ).astype(jnp.bfloat16)
    return jnp.dot(middle, out_weight, preferred_element_type=jnp.float32)


def per_device(
    strain_rows,
    bands,
    damaged,
    owner,
    first_layers,
    middle_weight,
    out_weight,
    band_scale,
    back_weight,
):
    count_all = lax.axis_size(("sec", "dev"))
    list_rows = damaged.shape[0]
    slot_count = max(2, 2 * list_rows // count_all)
    recv_rows = count_all * slot_count
    feat_width = strain_rows.shape[1]
    features = jnp.take(strain_rows, damaged, axis=0)
    band_local = jnp.take(bands, damaged)
    target_owner = owner[:, 0]
    matches = (target_owner[:, None] == jnp.arange(count_all, dtype=jnp.int32)[None, :]).astype(
        jnp.int32
    )
    slot_rank = jnp.sum((jnp.cumsum(matches, axis=0) - 1) * matches, axis=1)
    target = target_owner * slot_count + slot_rank
    dispatch = (jnp.arange(recv_rows, dtype=jnp.int32)[:, None] == target[None, :]).astype(
        jnp.bfloat16
    )
    send_band = jnp.dot(
        dispatch, band_local.astype(jnp.bfloat16)[:, None], preferred_element_type=jnp.float32
    ).astype(jnp.bfloat16)
    result = None
    for segment_index in range(PASSES):
        send_rows = jnp.dot(dispatch, features, preferred_element_type=jnp.float32).astype(
            jnp.bfloat16
        )
        got_rows, got_band = (
            lax.all_to_all(
                send_rows.reshape(count_all, slot_count, feat_width),
                ("sec", "dev"),
                split_axis=0,
                concat_axis=0,
                tiled=True,
            ),
            lax.all_to_all(
                send_band.reshape(count_all, slot_count),
                ("sec", "dev"),
                split_axis=0,
                concat_axis=0,
                tiled=True,
            ),
        )
        got_rows = got_rows.reshape(recv_rows, feat_width)
        got_band = got_band.reshape(recv_rows)
        hidden = first_hidden(got_rows, first_layers, got_band, band_scale)
        every_hidden = lax.all_gather(hidden, "sec", axis=0, tiled=True)
        partial_value = lax.psum_scatter(
            surrogate_tail(every_hidden, middle_weight, out_weight),
            "sec",
            scatter_dimension=0,
            tiled=True,
        )
        response = partial_value.astype(jnp.bfloat16)
        returned = lax.all_to_all(
            response.reshape(count_all, slot_count, response.shape[1]),
            ("sec", "dev"),
            split_axis=0,
            concat_axis=0,
            tiled=True,
        )
        returned = returned.reshape(recv_rows, response.shape[1])
        result = lax.dot_general(
            dispatch, returned, (((0,), (0,)), ((), ())), preferred_element_type=jnp.float32
        ).astype(jnp.bfloat16)
        if segment_index + 1 < PASSES:
            features = (
                features.astype(jnp.float32)
                + jnp.dot(result, back_weight, preferred_element_type=jnp.float32)
            ).astype(jnp.bfloat16)
    return result


def solution(mesh):
    in_specs = (
        P(("sec", "dev"), None),
        P(("sec", "dev")),
        P(("sec", "dev")),
        P(("sec", "dev"), None),
        P(("sec", "dev"), None),
        P(None, "sec"),
        P("sec", None),
        P(),
        P(),
    )
    out_specs = P(("sec", "dev"), None)
    return jax.shard_map(
        per_device, mesh=mesh, in_specs=in_specs, out_specs=out_specs, check_vma=False
    )
```

profile of v0, /device:TPU:1, one launch (start us, length us, event | category | flops | bytes accessed | tf_op | source)
XLA Modules:
  0.0 353.5 jit_solution(7108966665682831879)
XLA Ops:
  6.5 0.0 copy-start
  6.5 0.7 compare_select_fusion
  7.3 0.7 fusion.12
  8.0 0.2 reduce_window_sum.11
  8.2 0.8 select_reduce_fusion
  9.0 0.7 multiply_add_fusion
  9.7 1.6 gather_fusion.1
  11.3 0.8 fusion.3
  12.1 0.8 all_to_all.25
  13.0 11.5 %all-to-all-start.1 = ((bf16[128,1,2]{2,1,0:T(2,128)(2,1)}), bf16[128,1,2]{2,1,0:T(2,128)(2,1)S(1)}, u32[]{:S(2)}, u32[]{:S(2)}) async-start(bf16[128,1,2]{2,1,0:T(2,128)(2,1)} %all_to_all.25), calls=%async_computation.1 | async-start | bytes 131072 | tf_op jit(solution)/shard_map/all_to_all | solution.py:74
  24.5 0.7 compare_and_fusion
  25.1 1.8 gather_fusion
  26.9 0.8 convolution_convert_fusion.1
  27.7 6.2 %all-to-all-done.1 = bf16[128,1,2]{2,1,0:T(2,128)(2,1)S(1)} async-done(((bf16[128,1,2]{2,1,0:T(2,128)(2,1)}), bf16[128,1,2]{2,1,0:T(2,128)(2,1)S(1)}, u32[]{:S(2)}, u32[]{:S(2)}) %all-to-all-start.1) | async-done | bytes 544 | tf_op jit(solution)/shard_map/all_to_all | solution.py:74
  34.0 4.6 %all-to-all-start = ((bf16[128,2,128]{2,1,0:T(2,128)(2,1)}), bf16[128,2,128]{2,1,0:T(2,128)(2,1)S(1)}, u32[]{:S(2)}, u32[]{:S(2)}) async-start(bf16[128,2,128]{2,1,0:T(2,128)(2,1)} %bitcast.1), calls=%async_computation | async-start | bytes 131072 | tf_op jit(solution)/shard_map/all_to_all | solution.py:67
  38.6 0.0 all-gather.3.cloned.1.call-start
  38.6 0.2 convert_reduce_fusion
  38.8 0.1 reshape.65
  39.0 4.7 %fusion.4 = f32[256,4096]{1,0:T(8,128)} fusion(f32[16,4096]{1,0:T(8,128)} %param.16, f32[256]{0:T(256)S(1)} %reshape.65), kind=kOutput, calls=%fused_computation.19 | convolution fusion | flops 201330688 | bytes 4457472 | tf_op jit(solution)/shard_map/dot_general | solution.py:12
  43.7 4.4 %all-to-all-done = bf16[128,2,128]{2,1,0:T(2,128)(2,1)S(1)} async-done(((bf16[128,2,128]{2,1,0:T(2,128)(2,1)}), bf16[128,2,128]{2,1,0:T(2,128)(2,1)S(1)}, u32[]{:S(2)}, u32[]{:S(2)}) %all-to-all-start) | async-done | bytes 65568 | tf_op jit(solution)/shard_map/all_to_all | solution.py:67
  48.1 0.0 copy-done
  48.1 0.0 copy-start.1
  48.1 5.0 %multiply_convert_fusion.3 = bf16[256,4096]{1,0:T(8,128)(2,1)} fusion(f32[256,4096]{1,0:T(8,128)} %fusion.4, bf16[256,128]{1,0:T(8,128)(2,1)S(1)} %bitcast.33, bf16[128,4096]{1,0:T(8,128)(2,1)S(1)} %copy-done), kind=kOutput, calls=%fused_computation.7 | convolution fusion | flops 274726912 | bytes 7405568 | tf_op jit(solution)/shard_map/dot_general | solution.py:18
  53.0 0.0 all-gather.3.cloned.1.call-update
  53.1 0.0 copy-start.2
  53.1 0.2 reduce-scatter.3.cloned.1.call-start
  53.3 80.1 %all-gather.3.cloned.1.call-done = bf16[1024,4096]{1,0:T(8,128)(2,1)} async-done(((bf16[256,4096]{1,0:T(8,128)(2,1)}), bf16[1024,4096]{1,0:T(8,128)(2,1)}) %all-gather.3.cloned.1.call-update) | async-done | bytes 8388624 | tf_op jit(solution)/shard_map/all_gather | solution.py:85
  133.4 0.0 copy-done.1
  133.4 16.1 %fusion = f32[1024,128]{1,0:T(8,128)} fusion(bf16[1024,128]{1,0:T(8,128)(2,1)S(1)} %copy-done.1, bf16[1024,4096]{1,0:T(8,128)(2,1)} %all-gather.3.cloned.1.call-done, bf16[4096,1024]{1,0:T(8,128)(2,1)} %param.14), kind=kOutput, calls=%fused_computation.8 | convolution fusion | flops 8863612928 | bytes 17563648 | tf_op jit(solution)/shard_map/dot_general | solution.py:28
  149.5 0.0 reduce-scatter.3.cloned.1.call-update
  149.5 0.0 all-gather.5.cloned.1.call-start
  149.6 20.8 %reduce-scatter.3.cloned.1.call-done = f32[256,128]{1,0:T(8,128)} async-done(((f32[1024,128]{1,0:T(8,128)}), f32[256,128]{1,0:T(8,128)}) %reduce-scatter.3.cloned.1.call-update) | async-done | bytes 131088 | tf_op jit(solution)/shard_map/reduce_scatter | solution.py:86
  170.4 0.9 convert_element_type.71
  171.3 19.0 %all_to_all.31 = bf16[128,2,128]{2,1,0:T(2,128)(2,1)S(1)} all-to-all(bf16[128,2,128]{2,1,0:T(2,128)(2,1)S(1)} %bitcast.29), channel_id=1, replica_groups=mesh['sec'=4,'dev'=32] {'sec','dev'}, dimensions={0} | all-to-all | bytes 131072 | tf_op jit(solution)/shard_map/all_to_all | solution.py:93
  190.3 0.0 copy-done.2
  190.3 0.3 fusion.2
  190.6 0.2 convolution_convert_fusion
  190.8 13.9 %all_to_all.32 = bf16[128,2,128]{2,1,0:T(2,128)(2,1)S(1)} all-to-all(bf16[128,2,128]{2,1,0:T(2,128)(2,1)S(1)} %bitcast.32), channel_id=1, replica_groups=mesh['sec'=4,'dev'=32] {'sec','dev'}, dimensions={0} | all-to-all | bytes 131072 | tf_op jit(solution)/shard_map/all_to_all | solution.py:67
  204.7 4.9 %multiply_convert_fusion.1 = bf16[256,4096]{1,0:T(8,128)(2,1)} fusion(f32[256,4096]{1,0:T(8,128)} %fusion.4, bf16[256,128]{1,0:T(8,128)(2,1)S(1)} %bitcast.35, bf16[128,4096]{1,0:T(8,128)(2,1)S(1)} %copy-done), kind=kOutput, calls=%fused_computation.5 | convolution fusion | flops 274726912 | bytes 7405568 | tf_op jit(solution)/shard_map/dot_general | solution.py:18
  209.6 0.0 all-gather.5.cloned.1.call-update
  209.7 0.3 reduce-scatter.5.cloned.1.call-start
  209.9 79.3 %all-gather.5.cloned.1.call-done = bf16[1024,4096]{1,0:T(8,128)(2,1)} async-done(((bf16[256,4096]{1,0:T(8,128)(2,1)}), bf16[1024,4096]{1,0:T(8,128)(2,1)}) %all-gather.5.cloned.1.call-update) | async-done | bytes 8388624 | tf_op jit(solution)/shard_map/all_gather | solution.py:85
  289.2 16.1 %fusion.1 = f32[1024,128]{1,0:T(8,128)} fusion(bf16[1024,128]{1,0:T(8,128)(2,1)S(1)} %copy-done.1, bf16[1024,4096]{1,0:T(8,128)(2,1)} %all-gather.5.cloned.1.call-done, bf16[4096,1024]{1,0:T(8,128)(2,1)} %param.14), kind=kOutput, calls=%fused_computation.9 | convolution fusion | flops 8863612928 | bytes 17563648 | tf_op jit(solution)/shard_map/dot_general | solution.py:28
  305.4 0.0 reduce-scatter.5.cloned.1.call-update
  305.4 20.9 %reduce-scatter.5.cloned.1.call-done = f32[256,128]{1,0:T(8,128)} async-done(((f32[1024,128]{1,0:T(8,128)}), f32[256,128]{1,0:T(8,128)}) %reduce-scatter.5.cloned.1.call-update) | async-done | bytes 131088 | tf_op jit(solution)/shard_map/reduce_scatter | solution.py:86
  326.2 0.9 convert_element_type.77
  327.1 19.0 %all_to_all.33 = bf16[128,2,128]{2,1,0:T(2,128)(2,1)S(1)} all-to-all(bf16[128,2,128]{2,1,0:T(2,128)(2,1)S(1)} %bitcast.30), channel_id=1, replica_groups=mesh['sec'=4,'dev'=32] {'sec','dev'}, dimensions={0} | all-to-all | bytes 131072 | tf_op jit(solution)/shard_map/all_to_all | solution.py:93
  346.1 0.8 convolution_convert_fusion.2
  (2 shorter events, 0.0 us)
Async XLA Ops:
  6.5 41.5 %copy-start = (bf16[128,4096]{1,0:T(8,128)(2,1)S(1)}, bf16[128,4096]{1,0:T(8,128)(2,1)}, u32[]{:S(2)}) copy-start(bf16[128,4096]{1,0:T(8,128)(2,1)} %param.13) | copy-start | bytes 3145732
  13.0 21.0 %all-to-all-start.1 = ((bf16[128,1,2]{2,1,0:T(2,128)(2,1)}), bf16[128,1,2]{2,1,0:T(2,128)(2,1)S(1)}, u32[]{:S(2)}, u32[]{:S(2)}) async-start(bf16[128,1,2]{2,1,0:T(2,128)(2,1)} %all_to_all.25), calls=%async_computation.1 | async-start | bytes 131072 | tf_op jit(solution)/shard_map/all_to_all | solution.py:74
  34.0 14.1 %all-to-all-start = ((bf16[128,2,128]{2,1,0:T(2,128)(2,1)}), bf16[128,2,128]{2,1,0:T(2,128)(2,1)S(1)}, u32[]{:S(2)}, u32[]{:S(2)}) async-start(bf16[128,2,128]{2,1,0:T(2,128)(2,1)} %bitcast.1), calls=%async_computation | async-start | bytes 131072 | tf_op jit(solution)/shard_map/all_to_all | solution.py:67
  38.6 94.9 %all-gather.3.cloned.1.call-start = ((), (), s32[]{:S(2)}) async-start(), calls=%async_computation.7 | async-start | bytes 10485760 | tf_op jit(solution)/shard_map/all_gather | solution.py:85
  48.1 85.4 %copy-start.1 = (bf16[1024,128]{1,0:T(8,128)(2,1)S(1)}, bf16[1024,128]{1,0:T(8,128)(2,1)}, u32[]{:S(2)}) copy-start(bf16[1024,128]{1,0:T(8,128)(2,1)} %param.15) | copy-start | bytes 786436
  53.1 137.2 %copy-start.2 = (bf16[128,128]{1,0:T(8,128)(2,1)S(1)}, bf16[128,128]{1,0:T(8,128)(2,1)}, u32[]{:S(2)}) copy-start(bf16[128,128]{1,0:T(8,128)(2,1)} %param.17) | copy-start | bytes 98308
  53.1 117.3 %reduce-scatter.3.cloned.1.call-start = ((), (), s32[]{:S(2)}) async-start(), calls=%async_computation.8 | async-start | bytes 655360 | tf_op jit(solution)/shard_map/reduce_scatter | solution.py:86
  149.5 139.7 %all-gather.5.cloned.1.call-start = ((), (), s32[]{:S(2)}) async-start(), calls=%async_computation.9 | async-start | bytes 10485760 | tf_op jit(solution)/shard_map/all_gather | solution.py:85
  209.7 116.6 %reduce-scatter.5.cloned.1.call-start = ((), (), s32[]{:S(2)}) async-start(), calls=%async_computation.10 | async-start | bytes 655360 | tf_op jit(solution)/shard_map/reduce_scatter | solution.py:86
Sparse Core Ops, SparseCore 0:
  53.2 80.2 all-gather.2
  149.7 20.6 reduce-scatter.2
  209.8 79.4 all-gather.4
  305.5 20.6 reduce-scatter.4
where the time goes:
time: 354 us; the launch traced here: 353 us
  waiting for transfers between devices  212 us (60%)
  blocking collectives  51.9 us (15%)
  matrix products  49.8 us (14%)
  starting transfers between devices  16.7 us (5%)
  between operations  13.2 us (4%)
  other arithmetic  5.83 us (2%)
  local copies, waits for them, and re-layouts  4.35 us (1%)
    all_gather x2, waiting for transfers between devices, per_device(): every_hidden = lax.all_gather(hidden, 'sec', axis=0, tiled=True)  159 us
    reduce_scatter x2, waiting for transfers between devices, per_device(): lax.psum_scatter(surrogate_tail(every_hidden, middle_weight, out_weight),...  41.6 us
    all_to_all x2, blocking collectives, per_device(): lax.all_to_all(response.reshape(count_all, slot_count, response.shape[1])...  38 us
    dot_general x2, matrix products, surrogate_tail(): return jnp.dot(middle, out_weight, preferred_element_type=jnp.float32)  32.2 us
    all_to_all x1, blocking collectives, per_device(): lax.all_to_all(send_rows.reshape(count_all, slot_count, feat_width), ('se...  13.9 us
    all_to_all x1, starting transfers between devices, per_device(): lax.all_to_all(send_band.reshape(count_all, slot_count), ('sec', 'dev'),...  11.5 us
    dot_general x2, matrix products, first_hidden(): jnp.dot(row_block, weight_block, preferred_element_type=jnp.float32)  9.91 us
  transfers between devices with their start and end apart: 6, of which 6 were waited for; matrix products, arithmetic and copies ran while one was open for 2% of the time, Pallas kernels for 0%

commit v1 on v0

v1 whole, which is shorter than its diff:
```python
import functools

import jax
import jax.numpy as jnp
from jax import lax
from jax.experimental import pallas as pl
from jax.experimental.pallas import tpu as pltpu
from jax.sharding import PartitionSpec as P

MESH = pl.DeviceIdType.MESH
BF = jnp.bfloat16
F32 = jnp.float32
CHUNKS = 4


def iota(shape, axis):
    return lax.broadcasted_iota(jnp.int32, shape, axis)


def mm(a, b):
    return jnp.dot(a, b, preferred_element_type=F32)


def hot(cond):
    return jnp.where(cond, 1.0, 0.0).astype(BF)


def half_silu(u):
    return u + u * jnp.tanh(u)


def wait_bytes(ref, sem):
    pltpu.make_async_copy(ref, ref, sem).wait()


def kernel(
    nx,
    nd,
    strain_hbm,
    bands_ref,
    damaged_ref,
    owner_ref,
    w1_hbm,
    w2_hbm,
    outw_ref,
    scale_ref,
    back_ref,
    out_ref,
    strain_v,
    w1_v,
    w2_v,
    scale_v,
    scales_v,
    gather_v,
    dispatch_v,
    combine_v,
    feats_v,
    x0_v,
    x1_v,
    s0_v,
    s1_v,
    a0_v,
    a1_v,
    xw_v,
    h_v,
    acc_v,
    r0_v,
    r1_v,
    t0_v,
    t1_v,
    y0_v,
    y1_v,
    local_sem,
    w1own_sem,
    w1send_sem,
    w1recv_sem,
    send_sem,
    recv_sem,
):
    x = lax.axis_index("sec")
    d = lax.axis_index("dev")
    barrier = pltpu.get_barrier_semaphore()
    n = 128
    ch = w1_v.shape[3]
    right, left = lax.rem(x + 1, nx), lax.rem(x + nx - 1, nx)

    def at_x(k):
        return lax.rem(x + k, nx)

    for k in range(1, nx):
        pl.semaphore_signal(barrier, inc=1, device_id=(at_x(k), d), device_id_type=MESH)

    @pl.loop(1, nd)
    def _(i):
        pl.semaphore_signal(
            barrier, inc=1, device_id=(x, lax.rem(d + i, nd)), device_id_type=MESH
        )

    strain_copy = pltpu.make_async_copy(strain_hbm, strain_v, local_sem.at[0])
    strain_copy.start()
    w2_copy = pltpu.make_async_copy(w2_hbm, w2_v, local_sem.at[1])
    w2_copy.start()
    own_copies = []
    for c in range(CHUNKS):
        own = pltpu.make_async_copy(
            w1_hbm.at[:, pl.ds(c * ch, ch)], w1_v.at[c, 0], w1own_sem.at[c]
        )
        own.start()
        own_copies.append(own)

    eye = iota((n, n), 0) == iota((n, n), 1)
    ones = jnp.ones((n, n), BF)

    def spread(row):
        return mm(jnp.where(eye, row, 0.0).astype(BF), ones)

    damaged = damaged_ref[...]
    high = spread((damaged // n).astype(F32))
    low = spread((damaged % n).astype(F32))
    lane = iota((n, n), 1).astype(F32)
    on_low = low == lane
    band_part = jnp.zeros((n, n), F32)
    for b in range(strain_v.shape[0] // n):
        picked = jnp.logical_and(on_low, high == float(b))
        gather_v[:, b * n : (b + 1) * n] = hot(picked)
        band_part += jnp.where(picked, bands_ref[b : b + 1, :].astype(F32), 0.0)
    band_spread = mm(band_part.astype(BF), ones)
    band_row = jnp.sum(jnp.where(eye, band_spread, 0.0), axis=0, keepdims=True)
    owner_row = owner_ref[...].astype(F32)
    earlier = jnp.logical_and(
        spread(owner_row) == owner_row, iota((n, n), 0) < iota((n, n), 1)
    )
    rank = jnp.sum(jnp.where(earlier, 1.0, 0.0), axis=0, keepdims=True)
    target_row = 2.0 * owner_row + rank
    meta_at = iota((16, n), 0)
    x0_v[0, n : n + 16, :] = jnp.where(
        meta_at == 0, target_row, jnp.where(meta_at == 1, band_row, 0.0)
    ).astype(BF)
    strain_copy.wait()
    feats = mm(gather_v[...], strain_v[...])
    feats_v[...] = feats
    x0_v[0, 0:n, :] = feats.astype(BF)

    half = scale_ref[...] * 0.5
    term0 = half.astype(BF)
    rest = half - term0.astype(F32)
    term1 = rest.astype(BF)
    term2 = (rest - term1.astype(F32)).astype(BF)
    scale_v[0:16, :] = term0
    scale_v[16:32, :] = term1
    scale_v[32:48, :] = term2
    scale_v[48:128, :] = jnp.zeros((80, scale_v.shape[1]), BF)

    pl.semaphore_wait(barrier, nx - 1 + nd - 1)

    def send_along_x(src_of, dst, sem):
        for k in range(1, nx):
            pltpu.make_async_remote_copy(
                src_ref=src_of(k),
                dst_ref=dst.at[(nx - k) % nx],
                send_sem=send_sem.at[sem],
                recv_sem=recv_sem.at[sem],
                device_id=(at_x(k), d),
                device_id_type=MESH,
            ).start()

    def send_all(src, dst, sem):
        @pl.loop(1, nd)
        def _(i):
            to = lax.rem(d + i, nd)
            pltpu.make_async_remote_copy(
                src_ref=src.at[to],
                dst_ref=dst.at[d],
                send_sem=send_sem.at[sem],
                recv_sem=recv_sem.at[sem],
                device_id=(x, to),
                device_id_type=MESH,
            ).start()

        dst[pl.ds(d, 1)] = src[pl.ds(d, 1)]

    send_along_x(lambda k: x0_v.at[0], x0_v, 0)

    def w1_copy(src, c, slot, to, sem):
        return pltpu.make_async_remote_copy(
            src_ref=src,
            dst_ref=w1_v.at[c, slot],
            send_sem=w1send_sem.at[sem, c],
            recv_sem=w1recv_sem.at[slot, c],
            device_id=(to, d),
            device_id_type=MESH,
        )

    w1_copies = {}
    for c in range(CHUNKS):
        src = w1_hbm.at[:, pl.ds(c * ch, ch)]
        w1_copies[1, c] = w1_copy(src, c, 1, left, 0)
        w1_copies[3, c] = w1_copy(src, c, 3, right, 1)
        w1_copies[1, c].start()
        w1_copies[3, c].start()
        if c % 2 == 0:
            w1_copies[2, c] = w1_copy(w1_v.at[c, 3], c, 2, right, 2)
        else:
            w1_copies[2, c] = w1_copy(w1_v.at[c, 1], c, 2, left, 2)

    rows = nd * 32
    wait_bytes(x0_v.at[pl.ds(1, nx - 1)], recv_sem.at[0])

    def slot_code(at):
        dest, owner_at = at // 32, (at // 8) % 4
        lister, slot = (at // 2) % 4, at % 2
        code = (lax.rem(x + owner_at, nx) * nd + dest) * 2 + slot
        return code, lister

    down, down_lister = slot_code(iota((rows, n), 0))
    along, along_lister = slot_code(iota((n, rows), 1))
    band_cols = []
    for j in range(nx):
        meta = x0_v[j, n : n + 16, :].astype(F32)
        target_j, band_j = meta[0:1, :], meta[1:2, :]
        dispatch_v[:, j * n : (j + 1) * n] = hot(
            jnp.where(down_lister == j, down, -1).astype(F32) == target_j
        )
        target_down = spread(target_j)
        for b in range(rows // n):
            cut = slice(b * n, (b + 1) * n)
            combine_v[j * n : (j + 1) * n, cut] = hot(
                jnp.where(along_lister[:, cut] == j, along[:, cut], -1).astype(F32)
                == target_down
            )
        band_cols.append(spread(band_j).astype(BF))
    bands_all = jnp.concatenate(band_cols, axis=0)

    def spread_rows(features):
        return mm(dispatch_v[...], features).astype(BF).reshape(nd, 32, n)

    s0_v[:, 0:32, :] = spread_rows(x0_v[:, 0:n, :].reshape(nx * n, n))
    s0_v[:, 32:64, :] = spread_rows(bands_all)
    send_all(s0_v, a0_v, 1)
    wait_bytes(a0_v.at[pl.ds(0, nd - 1)], recv_sem.at[1])

    pair_rows = nd * 16
    level = iota((pair_rows, n), 1)
    level_of = jnp.where(level < 48, level % 16, -1).astype(F32)
    for p in range(2):
        got = a0_v[:, 32 + 16 * p : 48 + 16 * p, :].reshape(pair_rows, n).astype(F32)
        picks = hot(got == level_of)

        @pl.loop(0, scale_v.shape[1] // 256)
        def _(t):
            cols = pl.ds(pl.multiple_of(t * 256, 256), 256)
            scales_v[p, :, cols] = mm(picks, scale_v[:, cols])

    def widen(got, p):
        which = (iota((pair_rows, n), 0) // 8) % 2
        value = got[:, 16 * p : 16 * p + 16, :].reshape(pair_rows, n)
        zero = jnp.zeros_like(value)
        xw_v[p, :, 0:n] = jnp.where(which == 0, value, zero)
        xw_v[p, :, n : 2 * n] = jnp.where(which == 1, value, zero)

    def chunk(p, c):
        @pl.loop(0, ch // 256)
        def _(t):
            cols = pl.ds(pl.multiple_of(t * 256, 256), 256)
            across = pl.ds(pl.multiple_of(c * ch + t * 256, 256), 256)
            layer = w1_v[c, 2 * p : 2 * p + 2, :, cols].reshape(2 * n, 256)
            u = mm(xw_v[p], layer) * scales_v[p, :, across]
            h_v[:, cols] = half_silu(u).astype(BF)

        @pl.loop(0, w2_v.shape[1] // 256)
        def _(t):
            cols = pl.ds(pl.multiple_of(t * 256, 256), 256)
            part = mm(h_v[...], w2_v[c * ch : (c + 1) * ch, cols])
            if c == 0:
                acc_v[p, :, cols] = part
            else:
                acc_v[p, :, cols] += part

    def tail(p, dst):
        total = jnp.zeros((pair_rows, n), F32)
        for t in range(w2_v.shape[1] // 256):
            cols = slice(t * 256, (t + 1) * 256)
            middle = half_silu(acc_v[p, :, cols] * 0.5).astype(BF)
            total += mm(middle, outw_ref[cols, :])
        dst[:, 16 * p : 16 * p + 16, :] = total.astype(BF).reshape(nd, 16, n)

    def give_back(r_v, t_v, y_v, sem):
        send_all(r_v, t_v, sem)
        wait_bytes(t_v.at[pl.ds(0, nd - 1)], recv_sem.at[sem])
        points = mm(combine_v[...], t_v[...].reshape(rows, n))
        y_v[...] = points.astype(BF).reshape(nx, n, n)

    def sum_along_x(y_v, y_in, sem):
        send_along_x(lambda k: y_v.at[k], y_in, sem)
        wait_bytes(y_in.at[pl.ds(1, nx - 1)], recv_sem.at[sem])
        total = y_v[0].astype(F32)
        for k in range(1, nx):
            total += y_in[k].astype(F32)
        return total.astype(BF)

    for p in range(2):
        widen(a0_v[:, 0:32, :], p)
    w2_copy.wait()
    for c in range(CHUNKS):
        own_copies[c].wait()
        w1_copies[1, c].wait_recv()
        w1_copies[3, c].wait_recv()
        w1_copies[2, c].start()
        chunk(0, c)
    tail(0, r0_v)
    for c in range(CHUNKS):
        w1_copies[2, c].wait_recv()
        chunk(1, c)
    tail(1, r0_v)
    give_back(r0_v, t0_v, y0_v.at[0], 2)
    values = sum_along_x(y0_v.at[0], y0_v.at[1], 3)
    features = (feats_v[...] + mm(values, back_ref[...])).astype(BF)

    x1_v[0] = features
    send_along_x(lambda k: x1_v.at[0], x1_v, 4)
    wait_bytes(x1_v.at[pl.ds(1, nx - 1)], recv_sem.at[4])
    s1_v[...] = spread_rows(x1_v[...].reshape(nx * n, n))
    send_all(s1_v, a1_v, 5)
    wait_bytes(a1_v.at[pl.ds(0, nd - 1)], recv_sem.at[5])
    for p in range(2):
        widen(a1_v[...], p)
    for p in range(2):
        for c in range(CHUNKS):
            chunk(p, c)
        tail(p, r1_v)
    give_back(r1_v, t1_v, y1_v.at[0], 6)
    out_ref[...] = sum_along_x(y1_v.at[0], y1_v.at[1], 7)

    for copy in w1_copies.values():
        copy.wait_send()
    wait_bytes(x0_v.at[pl.ds(1, nx - 1)], send_sem.at[0])
    wait_bytes(a0_v.at[pl.ds(0, nd - 1)], send_sem.at[1])
    wait_bytes(t0_v.at[pl.ds(0, nd - 1)], send_sem.at[2])
    wait_bytes(y0_v.at[1, pl.ds(1, nx - 1)], send_sem.at[3])
    wait_bytes(x1_v.at[pl.ds(1, nx - 1)], send_sem.at[4])
    wait_bytes(a1_v.at[pl.ds(0, nd - 1)], send_sem.at[5])
    wait_bytes(t1_v.at[pl.ds(0, nd - 1)], send_sem.at[6])
    wait_bytes(y1_v.at[1, pl.ds(1, nx - 1)], send_sem.at[7])


def solution(mesh):
    nx, nd = mesh.shape["sec"], mesh.shape["dev"]

    def per_device(strain, bands, damaged, owner, w1, w2, outw, scale, back):
        n, hid = w1.shape
        points = strain.shape[0]
        mid = w2.shape[1]
        rows = nd * 32
        vmem = pl.BlockSpec(memory_space=pltpu.VMEM)
        hbm = pl.BlockSpec(memory_space=pl.ANY)
        return pl.pallas_call(
            functools.partial(kernel, nx, nd),
            out_shape=jax.ShapeDtypeStruct((n, outw.shape[1]), BF),
            in_specs=[hbm, vmem, vmem, vmem, hbm, hbm, vmem, vmem, vmem],
            out_specs=vmem,
            scratch_shapes=[
                pltpu.VMEM((points, n), BF),
                pltpu.VMEM((CHUNKS, nx, n, hid // CHUNKS), BF),
                pltpu.VMEM((hid, mid), BF),
                pltpu.VMEM((n, hid), BF),
                pltpu.VMEM((2, rows // 2, hid), F32),
                pltpu.VMEM((n, points), BF),
                pltpu.VMEM((rows, nx * n), BF),
                pltpu.VMEM((nx * n, rows), BF),
                pltpu.VMEM((n, n), F32),
                pltpu.VMEM((nx, n + 16, n), BF),
                pltpu.VMEM((nx, n, n), BF),
                pltpu.VMEM((nd, 64, n), BF),
                pltpu.VMEM((nd, 32, n), BF),
                pltpu.VMEM((nd, 64, n), BF),
                pltpu.VMEM((nd, 32, n), BF),
                pltpu.VMEM((2, rows // 2, 2 * n), BF),
                pltpu.VMEM((rows // 2, hid // CHUNKS), BF),
                pltpu.VMEM((2, rows // 2, mid), F32),
                pltpu.VMEM((nd, 32, n), BF),
                pltpu.VMEM((nd, 32, n), BF),
                pltpu.VMEM((nd, 32, n), BF),
                pltpu.VMEM((nd, 32, n), BF),
                pltpu.VMEM((2, nx, n, n), BF),
                pltpu.VMEM((2, nx, n, n), BF),
                pltpu.SemaphoreType.DMA((2,)),
                pltpu.SemaphoreType.DMA((CHUNKS,)),
                pltpu.SemaphoreType.DMA((3, CHUNKS)),
                pltpu.SemaphoreType.DMA((nx, CHUNKS)),
                pltpu.SemaphoreType.DMA((8,)),
                pltpu.SemaphoreType.DMA((8,)),
            ],
            compiler_params=pltpu.CompilerParams(
                collective_id=0,
                has_side_effects=True,
                vmem_limit_bytes=62 * 2**20,
            ),
        )(
            strain,
            bands.reshape(points // n, n),
            damaged.reshape(1, n),
            owner.reshape(1, n),
            w1,
            w2,
            outw,
            scale,
            back,
        )

    both = ("sec", "dev")
    return jax.shard_map(
        per_device,
        mesh=mesh,
        in_specs=(
            P(both, None),
            P(both),
            P(both),
            P(both, None),
            P(both, None),
            P(None, "sec"),
            P("sec", None),
            P(),
            P(),
        ),
        out_specs=P(both, None),
        check_vma=False,
    )
```

time: 354 us -> 111 us (0.31)
  waiting for transfers between devices: 212 us -> 0 us
  Pallas kernels: 0 us -> 110 us
  blocking collectives: 51.9 us -> 0 us
  matrix products: 49.8 us -> 0 us
  starting transfers between devices: 16.7 us -> 0 us
  between operations: 13.2 us -> 0.01 us
  other arithmetic: 5.83 us -> 0 us
    all_gather x2 -> x0, waiting for transfers between devices: 159 us -> none  [per_device(): every_hidden = lax.all_gather(hidden, 'sec', axis=0, tiled=True)]
    pallas_call x0 -> x1, Pallas kernels: none -> 110 us  [per_device(): pl.pallas_call(functools.partial(kernel, nx, nd), out_shape=jax.ShapeDtyp...]
    all_to_all x3 -> x0, blocking collectives: 51.9 us -> none  [the longest x2 38 us: per_device(): lax.all_to_all(response.reshape(count_all, slot_count, response.shape[1])...]
    dot_general x10 -> x0, matrix products: 49.8 us -> none  [the longest x2 32.2 us: surrogate_tail(): return jnp.dot(middle, out_weight, preferred_element_type=jnp.float32)]
    reduce_scatter x2 -> x0, waiting for transfers between devices: 41.6 us -> none  [per_device(): lax.psum_scatter(surrogate_tail(every_hidden, middle_weight, out_weight),...]
    all_to_all x2 -> x0, starting transfers between devices: 16.1 us -> none  [the longest x1 11.5 us: per_device(): lax.all_to_all(send_band.reshape(count_all, slot_count), ('sec', 'dev'),...]
    all_to_all x2 -> x0, waiting for transfers between devices: 10.6 us -> none  [the longest x1 6.23 us: per_device(): lax.all_to_all(send_band.reshape(count_all, slot_count), ('sec', 'dev'),...]
  transfers between devices with their start and end apart: 6 -> 0, of which waited for: 6 -> 0; matrix products, arithmetic and copies ran while one was open for 2% -> 0% of each run, Pallas kernels for 0% -> 0%
where the time goes in v1:
time: 111 us
  Pallas kernels  110 us (99%)
  local copies, waits for them, and re-layouts  1.38 us (1%)
    pallas_call x1, Pallas kernels, per_device(): pl.pallas_call(functools.partial(kernel, nx, nd), out_shape=jax.ShapeDtyp...  110 us

profile of v1, /device:TPU:1, one launch (start us, length us, event | category | flops | bytes accessed | tf_op | source)
XLA Modules:
  0.0 111.2 jit_solution(15770831225076262662)
XLA Ops:
  0.0 109.8 %shard_map.91 = bf16[128,128]{1,0:T(8,128)(2,1)} custom-call(bf16[2048,128]{1,0:T(8,128)(2,1)} %strain_hbm.1, s32[16,128]{1,0:T(8,128)} %bitcast.3, s32[1,128]{1,0:T(1,128)} %bitcast.4, s32[1,128]{1,0:T(1,128)} %bitcast.5, bf16[128,4096]{1,0:T(8,128)(2,1)} %w1_hbm.1, bf16[4096,1024]{1,0:T(8,128)(2,1)} %w2_hbm.1, bf16[1024,128]{1,0:T(8,128)(2,1)} %outw_ref.1, ...), custom_call_target="tpu_custom_call" | custom-call | tf_op jit(solution)/shard_map/pallas_call | solution.py:356
  109.9 1.4 %copy.11 = bf16[128,128]{1,0:T(8,128)(2,1)} copy(bf16[128,128]{1,0:T(8,128)(2,1)} %shard_map.91) | data formatting | bytes 65536

commit v2 on v1

--- a/solution.py
+++ b/solution.py
@@ -36,6 +36,7 @@
 def kernel(
     nx,
     nd,
+    ne,
     strain_hbm,
     bands_ref,
     damaged_ref,
@@ -58,12 +59,14 @@
     x0_v,
     x1_v,
     s0_v,
+    z0_v,
     s1_v,
     a0_v,
     a1_v,
     xw_v,
     h_v,
     acc_v,
+    m_v,
     r0_v,
     r1_v,
     t0_v,
@@ -90,11 +93,19 @@
     for k in range(1, nx):
         pl.semaphore_signal(barrier, inc=1, device_id=(at_x(k), d), device_id_type=MESH)
 
-    @pl.loop(1, nd)
-    def _(i):
-        pl.semaphore_signal(
-            barrier, inc=1, device_id=(x, lax.rem(d + i, nd)), device_id_type=MESH
-        )
+    z, e = d // ne, d % ne
+    nz = nd // ne
+
+    def at_z(k):
+        return lax.rem(z + k, nz) * ne + e
+
+    def at_e(k):
+        return z * ne + lax.rem(e + k, ne)
+
+    for k in range(1, nz):
+        pl.semaphore_signal(barrier, inc=1, device_id=(x, at_z(k)), device_id_type=MESH)
+    for k in range(1, ne):
+        pl.semaphore_signal(barrier, inc=1, device_id=(x, at_e(k)), device_id_type=MESH)
 
     strain_copy = pltpu.make_async_copy(strain_hbm, strain_v, local_sem.at[0])
     strain_copy.start()
@@ -151,7 +162,7 @@
     scale_v[32:48, :] = term2
     scale_v[48:128, :] = jnp.zeros((80, scale_v.shape[1]), BF)
 
-    pl.semaphore_wait(barrier, nx - 1 + nd - 1)
+    pl.semaphore_wait(barrier, nx - 1 + nz - 1 + ne - 1)
 
     def send_along_x(src_of, dst, sem):
         for k in range(1, nx):
@@ -192,16 +203,22 @@
         )
 
     w1_copies = {}
-    for c in range(CHUNKS):
-        src = w1_hbm.at[:, pl.ds(c * ch, ch)]
-        w1_copies[1, c] = w1_copy(src, c, 1, left, 0)
-        w1_copies[3, c] = w1_copy(src, c, 3, right, 1)
-        w1_copies[1, c].start()
+    to_right = range(CHUNKS)
+    to_left = [(c + CHUNKS // 2) % CHUNKS for c in to_right]
+    for c, e_c in zip(to_right, to_left):
+        w1_copies[3, c] = w1_copy(w1_hbm.at[:, pl.ds(c * ch, ch)], c, 3, right, 1)
+        w1_copies[1, e_c] = w1_copy(w1_hbm.at[:, pl.ds(e_c * ch, ch)], e_c, 1, left, 0)
         w1_copies[3, c].start()
-        if c % 2 == 0:
-            w1_copies[2, c] = w1_copy(w1_v.at[c, 3], c, 2, right, 2)
-        else:
-            w1_copies[2, c] = w1_copy(w1_v.at[c, 1], c, 2, left, 2)
+        w1_copies[1, e_c].start()
+
+    def forward(i):
+        c, e_c = to_right[i], to_left[i]
+        w1_copies[3, c].wait_recv()
+        w1_copies[2, c] = w1_copy(w1_v.at[c, 3], c, 2, right, 2)
+        w1_copies[2, c].start()
+        w1_copies[1, e_c].wait_recv()
+        w1_copies[2, e_c] = w1_copy(w1_v.at[e_c, 1], e_c, 2, left, 2)
+        w1_copies[2, e_c].start()
 
     rows = nd * 32
     wait_bytes(x0_v.at[pl.ds(1, nx - 1)], recv_sem.at[0])
@@ -234,21 +251,42 @@
     def spread_rows(features):
         return mm(dispatch_v[...], features).astype(BF).reshape(nd, 32, n)
 
-    s0_v[:, 0:32, :] = spread_rows(x0_v[:, 0:n, :].reshape(nx * n, n))
-    s0_v[:, 32:64, :] = spread_rows(bands_all)
-    send_all(s0_v, a0_v, 1)
-    wait_bytes(a0_v.at[pl.ds(0, nd - 1)], recv_sem.at[1])
+    sent = spread_rows(x0_v[:, 0:n, :].reshape(nx * n, n))
+    s0_v[:, :, 0:32, :] = sent.reshape(nz, ne, 32, n)
+    s0_v[:, :, 32:64, :] = spread_rows(bands_all).reshape(nz, ne, 32, n)
+    for k in range(1, nz):
+        pltpu.make_async_remote_copy(
+            src_ref=s0_v.at[lax.rem(z + k, nz)],
+            dst_ref=z0_v.at[z],
+            send_sem=send_sem.at[1],
+            recv_sem=recv_sem.at[1],
+            device_id=(x, at_z(k)),
+            device_id_type=MESH,
+        ).start()
+    z0_v[pl.ds(z, 1)] = s0_v[pl.ds(z, 1)]
+    wait_bytes(z0_v.at[pl.ds(0, nz - 1)], recv_sem.at[1])
+    for k in range(1, ne):
+        pltpu.make_async_remote_copy(
+            src_ref=z0_v.at[:, lax.rem(e + k, ne)],
+            dst_ref=a0_v.at[:, e],
+            send_sem=send_sem.at[8],
+            recv_sem=recv_sem.at[8],
+            device_id=(x, at_e(k)),
+            device_id_type=MESH,
+        ).start()
+    a0_v[:, pl.ds(e, 1)] = z0_v[:, pl.ds(e, 1)]
+    wait_bytes(a0_v.at[:, pl.ds(0, ne - 1)], recv_sem.at[8])
+    for i in range(CHUNKS // 2):
+        forward(i)
 
     pair_rows = nd * 16
     level = iota((pair_rows, n), 1)
     level_of = jnp.where(level < 48, level % 16, -1).astype(F32)
     for p in range(2):
-        got = a0_v[:, 32 + 16 * p : 48 + 16 * p, :].reshape(pair_rows, n).astype(F32)
-        picks = hot(got == level_of)
-
-        @pl.loop(0, scale_v.shape[1] // 256)
-        def _(t):
-            cols = pl.ds(pl.multiple_of(t * 256, 256), 256)
+        got = a0_v[:, :, 32 + 16 * p : 48 + 16 * p, :].reshape(pair_rows, n)
+        picks = hot(got.astype(F32) == level_of)
+        for c in range(CHUNKS):
+            cols = slice(c * ch, (c + 1) * ch)
             scales_v[p, :, cols] = mm(picks, scale_v[:, cols])
 
     def widen(got, p):
@@ -258,33 +296,34 @@
         xw_v[p, :, 0:n] = jnp.where(which == 0, value, zero)
         xw_v[p, :, n : 2 * n] = jnp.where(which == 1, value, zero)
 
-    def chunk(p, c):
-        @pl.loop(0, ch // 256)
-        def _(t):
-            cols = pl.ds(pl.multiple_of(t * 256, 256), 256)
-            across = pl.ds(pl.multiple_of(c * ch + t * 256, 256), 256)
-            layer = w1_v[c, 2 * p : 2 * p + 2, :, cols].reshape(2 * n, 256)
-            u = mm(xw_v[p], layer) * scales_v[p, :, across]
-            h_v[:, cols] = half_silu(u).astype(BF)
-
+    def first(p, c):
+        cols = slice(c * ch, (c + 1) * ch)
+        layer = w1_v[c, 2 * p : 2 * p + 2].reshape(2 * n, ch)
+        u = mm(xw_v[p], layer) * scales_v[p, :, cols]
+        h_v[p * pair_rows : (p + 1) * pair_rows, cols] = half_silu(u).astype(BF)
+
+    def second(row, count, ranges, start, end):
         @pl.loop(0, w2_v.shape[1] // 256)
         def _(t):
             cols = pl.ds(pl.multiple_of(t * 256, 256), 256)
-            part = mm(h_v[...], w2_v[c * ch : (c + 1) * ch, cols])
-            if c == 0:
-                acc_v[p, :, cols] = part
+            part = None
+            for lo, hi in ranges:
+                term = mm(h_v[row : row + count, lo:hi], w2_v[lo:hi, cols])
+                part = term if part is None else part + term
+            if not start:
+                part += acc_v[0:count, cols]
+            if end:
+                m_v[row : row + count, cols] = half_silu(part * 0.5).astype(BF)
             else:
-                acc_v[p, :, cols] += part
-
-    def tail(p, dst):
-        total = jnp.zeros((pair_rows, n), F32)
-        for t in range(w2_v.shape[1] // 256):
-            cols = slice(t * 256, (t + 1) * 256)
-            middle = half_silu(acc_v[p, :, cols] * 0.5).astype(BF)
-            total += mm(middle, outw_ref[cols, :])
-        dst[:, 16 * p : 16 * p + 16, :] = total.astype(BF).reshape(nd, 16, n)
+                acc_v[0:count, cols] = part
+
+    def third(row, count):
+        total = mm(m_v[row : row + count, :], outw_ref[...])
+        return total.astype(BF).reshape(nd, 16, n)
 
     def give_back(r_v, t_v, y_v, sem):
+        for p in range(2):
+            r_v[:, 16 * p : 16 * p + 16, :] = third(p * pair_rows, pair_rows)
         send_all(r_v, t_v, sem)
         wait_bytes(t_v.at[pl.ds(0, nd - 1)], recv_sem.at[sem])
         points = mm(combine_v[...], t_v[...].reshape(rows, n))
@@ -299,19 +338,24 @@
         return total.astype(BF)
 
     for p in range(2):
-        widen(a0_v[:, 0:32, :], p)
+        widen(a0_v[...].reshape(nd, 64, n), p)
     w2_copy.wait()
-    for c in range(CHUNKS):
+    for i in range(CHUNKS):
+        c = to_left[i]
         own_copies[c].wait()
-        w1_copies[1, c].wait_recv()
-        w1_copies[3, c].wait_recv()
-        w1_copies[2, c].start()
-        chunk(0, c)
-    tail(0, r0_v)
-    for c in range(CHUNKS):
-        w1_copies[2, c].wait_recv()
-        chunk(1, c)
-    tail(1, r0_v)
+        if i >= CHUNKS // 2:
+            w1_copies[1, c].wait_recv()
+            w1_copies[3, to_right[i]].wait_recv()
+        first(0, c)
+    hid = w2_v.shape[0]
+    second(0, pair_rows, [(0, hid)], True, True)
+    for i in range(CHUNKS // 2):
+        ranges = []
+        for c in (to_right[i], to_left[i]):
+            w1_copies[2, c].wait_recv()
+            first(1, c)
+            ranges.append((c * ch, (c + 1) * ch))
+        second(pair_rows, pair_rows, ranges, i == 0, i == CHUNKS // 2 - 1)
     give_back(r0_v, t0_v, y0_v.at[0], 2)
     values = sum_along_x(y0_v.at[0], y0_v.at[1], 3)
     features = (feats_v[...] + mm(values, back_ref[...])).astype(BF)
@@ -324,17 +368,17 @@
     wait_bytes(a1_v.at[pl.ds(0, nd - 1)], recv_sem.at[5])
     for p in range(2):
         widen(a1_v[...], p)
-    for p in range(2):
         for c in range(CHUNKS):
-            chunk(p, c)
-        tail(p, r1_v)
+            first(p, c)
+    second(0, rows, [(0, hid)], True, True)
     give_back(r1_v, t1_v, y1_v.at[0], 6)
     out_ref[...] = sum_along_x(y1_v.at[0], y1_v.at[1], 7)
 
     for copy in w1_copies.values():
         copy.wait_send()
     wait_bytes(x0_v.at[pl.ds(1, nx - 1)], send_sem.at[0])
-    wait_bytes(a0_v.at[pl.ds(0, nd - 1)], send_sem.at[1])
+    wait_bytes(z0_v.at[pl.ds(0, nz - 1)], send_sem.at[1])
+    wait_bytes(a0_v.at[:, pl.ds(0, ne - 1)], send_sem.at[8])
     wait_bytes(t0_v.at[pl.ds(0, nd - 1)], send_sem.at[2])
     wait_bytes(y0_v.at[1, pl.ds(1, nx - 1)], send_sem.at[3])
     wait_bytes(x1_v.at[pl.ds(1, nx - 1)], send_sem.at[4])
@@ -345,6 +389,7 @@
 
 def solution(mesh):
     nx, nd = mesh.shape["sec"], mesh.shape["dev"]
+    ne = 8
 
     def per_device(strain, bands, damaged, owner, w1, w2, outw, scale, back):
         n, hid = w1.shape
@@ -354,7 +399,7 @@
         vmem = pl.BlockSpec(memory_space=pltpu.VMEM)
         hbm = pl.BlockSpec(memory_space=pl.ANY)
         return pl.pallas_call(
-            functools.partial(kernel, nx, nd),
+            functools.partial(kernel, nx, nd, ne),
             out_shape=jax.ShapeDtypeStruct((n, outw.shape[1]), BF),
             in_specs=[hbm, vmem, vmem, vmem, hbm, hbm, vmem, vmem, vmem],
             out_specs=vmem,
@@ -370,13 +415,15 @@
                 pltpu.VMEM((n, n), F32),
                 pltpu.VMEM((nx, n + 16, n), BF),
                 pltpu.VMEM((nx, n, n), BF),
-                pltpu.VMEM((nd, 64, n), BF),
-                pltpu.VMEM((nd, 32, n), BF),
-                pltpu.VMEM((nd, 64, n), BF),
+                pltpu.VMEM((nd // ne, ne, 64, n), BF),
+                pltpu.VMEM((nd // ne, ne, 64, n), BF),
+                pltpu.VMEM((nd, 32, n), BF),
+                pltpu.VMEM((nd // ne, ne, 64, n), BF),
                 pltpu.VMEM((nd, 32, n), BF),
                 pltpu.VMEM((2, rows // 2, 2 * n), BF),
-                pltpu.VMEM((rows // 2, hid // CHUNKS), BF),
-                pltpu.VMEM((2, rows // 2, mid), F32),
+                pltpu.VMEM((rows, hid), BF),
+                pltpu.VMEM((rows // 2, mid), F32),
+                pltpu.VMEM((rows, mid), BF),
                 pltpu.VMEM((nd, 32, n), BF),
                 pltpu.VMEM((nd, 32, n), BF),
                 pltpu.VMEM((nd, 32, n), BF),
@@ -387,8 +434,8 @@
                 pltpu.SemaphoreType.DMA((CHUNKS,)),
                 pltpu.SemaphoreType.DMA((3, CHUNKS)),
                 pltpu.SemaphoreType.DMA((nx, CHUNKS)),
-                pltpu.SemaphoreType.DMA((8,)),
-                pltpu.SemaphoreType.DMA((8,)),
+                pltpu.SemaphoreType.DMA((9,)),
+                pltpu.SemaphoreType.DMA((9,)),
             ],
             compiler_params=pltpu.CompilerParams(
                 collective_id=0,

time: 111 us -> 96.9 us (0.87)
  Pallas kernels: 110 us -> 95.3 us
    pallas_call x1, Pallas kernels: 110 us -> 95.3 us  [per_device(): pl.pallas_call(functools.partial(kernel, nx, nd, ne), out_shape=jax.Shape...]
where the time goes in v2:
time: 96.9 us; the launch traced here: 96.7 us
  Pallas kernels  95.3 us (98%)
  local copies, waits for them, and re-layouts  1.38 us (1%)
    pallas_call x1, Pallas kernels, per_device(): pl.pallas_call(functools.partial(kernel, nx, nd, ne), out_shape=jax.Shape...  95.3 us

profile of v2, /device:TPU:1, one launch (start us, length us, event | category | flops | bytes accessed | tf_op | source)
XLA Modules:
  0.0 96.7 jit_solution(16721241027323856780)
XLA Ops:
  0.0 95.3 %shard_map.91 = bf16[128,128]{1,0:T(8,128)(2,1)} custom-call(bf16[2048,128]{1,0:T(8,128)(2,1)} %strain_hbm.1, s32[16,128]{1,0:T(8,128)} %bitcast.3, s32[1,128]{1,0:T(1,128)} %bitcast.4, s32[1,128]{1,0:T(1,128)} %bitcast.5, bf16[128,4096]{1,0:T(8,128)(2,1)} %w1_hbm.1, bf16[4096,1024]{1,0:T(8,128)(2,1)} %w2_hbm.1, bf16[1024,128]{1,0:T(8,128)(2,1)} %outw_ref.1, ...), custom_call_target="tpu_custom_call" | custom-call | tf_op jit(solution)/shard_map/pallas_call | solution.py:401
  95.3 1.4 %copy.11 = bf16[128,128]{1,0:T(8,128)(2,1)} copy(bf16[128,128]{1,0:T(8,128)(2,1)} %shard_map.91) | data formatting | bytes 65536

commit v3 on v2

--- a/solution.py
+++ b/solution.py
@@ -10,7 +10,8 @@
 MESH = pl.DeviceIdType.MESH
 BF = jnp.bfloat16
 F32 = jnp.float32
-CHUNKS = 4
+CHUNKS = 8
+MSG = BF
 
 
 def iota(shape, axis):
@@ -55,14 +56,14 @@
     gather_v,
     dispatch_v,
     combine_v,
+    direct_v,
     feats_v,
     x0_v,
-    x1_v,
     s0_v,
     z0_v,
-    s1_v,
+    q1_v,
     a0_v,
-    a1_v,
+    u1_v,
     xw_v,
     h_v,
     acc_v,
@@ -71,8 +72,6 @@
     r1_v,
     t0_v,
     t1_v,
-    y0_v,
-    y1_v,
     local_sem,
     w1own_sem,
     w1send_sem,
@@ -175,20 +174,23 @@
                 device_id_type=MESH,
             ).start()
 
-    def send_all(src, dst, sem):
-        @pl.loop(1, nd)
+    def send_direct(src, dst, sem):
+        @pl.loop(1, nx * nd)
         def _(i):
-            to = lax.rem(d + i, nd)
+            to = lax.rem(x * nd + d + i, nx * nd)
+            to_x, to_d = to // nd, to % nd
+            off = lax.rem(to_x - x + nx, nx)
             pltpu.make_async_remote_copy(
-                src_ref=src.at[to],
-                dst_ref=dst.at[d],
+                src_ref=src.at[to_d * nx + off],
+                dst_ref=dst.at[d * nx + lax.rem(nx - off, nx)],
                 send_sem=send_sem.at[sem],
                 recv_sem=recv_sem.at[sem],
-                device_id=(x, to),
+                device_id=(to_x, to_d),
                 device_id_type=MESH,
             ).start()
 
-        dst[pl.ds(d, 1)] = src[pl.ds(d, 1)]
+        dst[pl.ds(d * nx, 1)] = src[pl.ds(d * nx, 1)]
+        wait_bytes(dst.at[pl.ds(0, nx * nd - 1)], recv_sem.at[sem])
 
     send_along_x(lambda k: x0_v.at[0], x0_v, 0)
 
@@ -223,14 +225,12 @@
     rows = nd * 32
     wait_bytes(x0_v.at[pl.ds(1, nx - 1)], recv_sem.at[0])
 
-    def slot_code(at):
-        dest, owner_at = at // 32, (at // 8) % 4
-        lister, slot = (at // 2) % 4, at % 2
-        code = (lax.rem(x + owner_at, nx) * nd + dest) * 2 + slot
-        return code, lister
-
-    down, down_lister = slot_code(iota((rows, n), 0))
-    along, along_lister = slot_code(iota((n, rows), 1))
+    def slot_code(dest, owner_at, slot):
+        return (lax.rem(x + owner_at, nx) * nd + dest) * 2 + slot
+
+    at = iota((rows, n), 0)
+    down = slot_code(at // 32, (at // 16) % 2 * 2 + (at // 2) % 2, at % 2)
+    down_lister = (at // 4) % 4
     band_cols = []
     for j in range(nx):
         meta = x0_v[j, n : n + 16, :].astype(F32)
@@ -238,13 +238,6 @@
         dispatch_v[:, j * n : (j + 1) * n] = hot(
             jnp.where(down_lister == j, down, -1).astype(F32) == target_j
         )
-        target_down = spread(target_j)
-        for b in range(rows // n):
-            cut = slice(b * n, (b + 1) * n)
-            combine_v[j * n : (j + 1) * n, cut] = hot(
-                jnp.where(along_lister[:, cut] == j, along[:, cut], -1).astype(F32)
-                == target_down
-            )
         band_cols.append(spread(band_j).astype(BF))
     bands_all = jnp.concatenate(band_cols, axis=0)
 
@@ -269,17 +262,25 @@
         pltpu.make_async_remote_copy(
             src_ref=z0_v.at[:, lax.rem(e + k, ne)],
             dst_ref=a0_v.at[:, e],
-            send_sem=send_sem.at[8],
-            recv_sem=recv_sem.at[8],
+            send_sem=send_sem.at[5],
+            recv_sem=recv_sem.at[5],
             device_id=(x, at_e(k)),
             device_id_type=MESH,
         ).start()
     a0_v[:, pl.ds(e, 1)] = z0_v[:, pl.ds(e, 1)]
-    wait_bytes(a0_v.at[:, pl.ds(0, ne - 1)], recv_sem.at[8])
-    for i in range(CHUNKS // 2):
-        forward(i)
-
+    wait_bytes(a0_v.at[:, pl.ds(0, ne - 1)], recv_sem.at[5])
+    direct_v[...] = hot(
+        slot_code(at // 32, (at // 8) % 4 + (at // 2) % 4, at % 2).astype(F32)
+        == target_row
+    )
+    at = iota((n, rows), 1)
+    combine_v[...] = hot(
+        slot_code(at // 32, (at // 8) % 4 + (at // 2) % 4, at % 2).astype(F32)
+        == jnp.concatenate([spread(target_row)] * (rows // n), axis=1)
+    )
     pair_rows = nd * 16
+    forward(0)
+    forward(1)
     level = iota((pair_rows, n), 1)
     level_of = jnp.where(level < 48, level % 16, -1).astype(F32)
     for p in range(2):
@@ -288,13 +289,20 @@
         for c in range(CHUNKS):
             cols = slice(c * ch, (c + 1) * ch)
             scales_v[p, :, cols] = mm(picks, scale_v[:, cols])
-
-    def widen(got, p):
-        which = (iota((pair_rows, n), 0) // 8) % 2
-        value = got[:, 16 * p : 16 * p + 16, :].reshape(pair_rows, n)
+        forward(2 + p)
+
+    def widen(value, p):
+        which = (iota((pair_rows, n), 0) // 2) % 2
         zero = jnp.zeros_like(value)
-        xw_v[p, :, 0:n] = jnp.where(which == 0, value, zero)
-        xw_v[p, :, n : 2 * n] = jnp.where(which == 1, value, zero)
+        xw_v[p, :, 0:n] = jnp.where(which == 0, value, zero).astype(BF)
+        xw_v[p, :, n : 2 * n] = jnp.where(which == 1, value, zero).astype(BF)
+
+    low_half = iota((rows // 16, 8, n), 1) < 4
+
+    def swap(one, two):
+        first_of = jnp.where(low_half, one, pltpu.roll(two, 4, axis=1))
+        second_of = jnp.where(low_half, pltpu.roll(one, 4, axis=1), two)
+        return first_of, second_of
 
     def first(p, c):
         cols = slice(c * ch, (c + 1) * ch)
@@ -317,28 +325,19 @@
             else:
                 acc_v[0:count, cols] = part
 
-    def third(row, count):
-        total = mm(m_v[row : row + count, :], outw_ref[...])
-        return total.astype(BF).reshape(nd, 16, n)
-
-    def give_back(r_v, t_v, y_v, sem):
+    def give_back(r_v, t_v, sem):
+        parts = []
         for p in range(2):
-            r_v[:, 16 * p : 16 * p + 16, :] = third(p * pair_rows, pair_rows)
-        send_all(r_v, t_v, sem)
-        wait_bytes(t_v.at[pl.ds(0, nd - 1)], recv_sem.at[sem])
-        points = mm(combine_v[...], t_v[...].reshape(rows, n))
-        y_v[...] = points.astype(BF).reshape(nx, n, n)
-
-    def sum_along_x(y_v, y_in, sem):
-        send_along_x(lambda k: y_v.at[k], y_in, sem)
-        wait_bytes(y_in.at[pl.ds(1, nx - 1)], recv_sem.at[sem])
-        total = y_v[0].astype(F32)
-        for k in range(1, nx):
-            total += y_in[k].astype(F32)
-        return total.astype(BF)
+            total = mm(m_v[p * pair_rows : (p + 1) * pair_rows, :], outw_ref[...])
+            parts.append(total.reshape(rows // 16, 8, n))
+        even, odd = swap(*parts)
+        r_v[...] = jnp.stack([even, odd], axis=1).reshape(rows // 8, 8, n).astype(MSG)
+        send_direct(r_v, t_v, sem)
+        return mm(combine_v[...], t_v[...].reshape(rows, n).astype(BF)).astype(BF)
 
     for p in range(2):
-        widen(a0_v[...].reshape(nd, 64, n), p)
+        got = a0_v[:, :, 16 * p : 16 * p + 16, :]
+        widen(got.reshape(pair_rows, n), p)
     w2_copy.wait()
     for i in range(CHUNKS):
         c = to_left[i]
@@ -356,35 +355,26 @@
             first(1, c)
             ranges.append((c * ch, (c + 1) * ch))
         second(pair_rows, pair_rows, ranges, i == 0, i == CHUNKS // 2 - 1)
-    give_back(r0_v, t0_v, y0_v.at[0], 2)
-    values = sum_along_x(y0_v.at[0], y0_v.at[1], 3)
+    values = give_back(r0_v, t0_v, 2)
     features = (feats_v[...] + mm(values, back_ref[...])).astype(BF)
 
-    x1_v[0] = features
-    send_along_x(lambda k: x1_v.at[0], x1_v, 4)
-    wait_bytes(x1_v.at[pl.ds(1, nx - 1)], recv_sem.at[4])
-    s1_v[...] = spread_rows(x1_v[...].reshape(nx * n, n))
-    send_all(s1_v, a1_v, 5)
-    wait_bytes(a1_v.at[pl.ds(0, nd - 1)], recv_sem.at[5])
-    for p in range(2):
-        widen(a1_v[...], p)
+    q1_v[...] = mm(direct_v[...], features).reshape(rows // 8, 8, n).astype(MSG)
+    send_direct(q1_v, u1_v, 3)
+    got = u1_v[...].astype(F32).reshape(rows // 16, 2, 8, n)
+    for p, value in enumerate(swap(got[:, 0], got[:, 1])):
+        widen(value.reshape(pair_rows, n), p)
         for c in range(CHUNKS):
             first(p, c)
     second(0, rows, [(0, hid)], True, True)
-    give_back(r1_v, t1_v, y1_v.at[0], 6)
-    out_ref[...] = sum_along_x(y1_v.at[0], y1_v.at[1], 7)
+    out_ref[...] = give_back(r1_v, t1_v, 4)
 
     for copy in w1_copies.values():
         copy.wait_send()
     wait_bytes(x0_v.at[pl.ds(1, nx - 1)], send_sem.at[0])
     wait_bytes(z0_v.at[pl.ds(0, nz - 1)], send_sem.at[1])
-    wait_bytes(a0_v.at[:, pl.ds(0, ne - 1)], send_sem.at[8])
-    wait_bytes(t0_v.at[pl.ds(0, nd - 1)], send_sem.at[2])
-    wait_bytes(y0_v.at[1, pl.ds(1, nx - 1)], send_sem.at[3])
-    wait_bytes(x1_v.at[pl.ds(1, nx - 1)], send_sem.at[4])
-    wait_bytes(a1_v.at[pl.ds(0, nd - 1)], send_sem.at[5])
-    wait_bytes(t1_v.at[pl.ds(0, nd - 1)], send_sem.at[6])
-    wait_bytes(y1_v.at[1, pl.ds(1, nx - 1)], send_sem.at[7])
+    wait_bytes(a0_v.at[:, pl.ds(0, ne - 1)], send_sem.at[5])
+    for dst, sem in ((t0_v, 2), (u1_v, 3), (t1_v, 4)):
+        wait_bytes(dst.at[pl.ds(0, nx * nd - 1)], send_sem.at[sem])
 
 
 def solution(mesh):
@@ -411,31 +401,29 @@
                 pltpu.VMEM((2, rows // 2, hid), F32),
                 pltpu.VMEM((n, points), BF),
                 pltpu.VMEM((rows, nx * n), BF),
-                pltpu.VMEM((nx * n, rows), BF),
+                pltpu.VMEM((n, rows), BF),
+                pltpu.VMEM((rows, n), BF),
                 pltpu.VMEM((n, n), F32),
                 pltpu.VMEM((nx, n + 16, n), BF),
-                pltpu.VMEM((nx, n, n), BF),
                 pltpu.VMEM((nd // ne, ne, 64, n), BF),
                 pltpu.VMEM((nd // ne, ne, 64, n), BF),
-                pltpu.VMEM((nd, 32, n), BF),
+                pltpu.VMEM((rows // 8, 8, n), MSG),
                 pltpu.VMEM((nd // ne, ne, 64, n), BF),
-                pltpu.VMEM((nd, 32, n), BF),
+                pltpu.VMEM((rows // 8, 8, n), MSG),
                 pltpu.VMEM((2, rows // 2, 2 * n), BF),
                 pltpu.VMEM((rows, hid), BF),
                 pltpu.VMEM((rows // 2, mid), F32),
                 pltpu.VMEM((rows, mid), BF),
-                pltpu.VMEM((nd, 32, n), BF),
-                pltpu.VMEM((nd, 32, n), BF),
-                pltpu.VMEM((nd, 32, n), BF),
-                pltpu.VMEM((nd, 32, n), BF),
-                pltpu.VMEM((2, nx, n, n), BF),
-                pltpu.VMEM((2, nx, n, n), BF),
+                pltpu.VMEM((rows // 8, 8, n), MSG),
+                pltpu.VMEM((rows // 8, 8, n), MSG),
+                pltpu.VMEM((rows // 8, 8, n), MSG),
+                pltpu.VMEM((rows // 8, 8, n), MSG),
                 pltpu.SemaphoreType.DMA((2,)),
                 pltpu.SemaphoreType.DMA((CHUNKS,)),
                 pltpu.SemaphoreType.DMA((3, CHUNKS)),
                 pltpu.SemaphoreType.DMA((nx, CHUNKS)),
-                pltpu.SemaphoreType.DMA((9,)),
-                pltpu.SemaphoreType.DMA((9,)),
+                pltpu.SemaphoreType.DMA((6,)),
+                pltpu.SemaphoreType.DMA((6,)),
             ],
             compiler_params=pltpu.CompilerParams(
                 collective_id=0,

time: 96.9 us -> 92.5 us (0.955)
  Pallas kernels: 95.3 us -> 90.9 us
    pallas_call x1, Pallas kernels: 95.3 us -> 90.9 us  [per_device(): pl.pallas_call(functools.partial(kernel, nx, nd, ne), out_shape=jax.Shape...]
where the time goes in v3:
time: 92.5 us; the launch traced here: 92.3 us
  Pallas kernels  90.9 us (98%)
  local copies, waits for them, and re-layouts  1.38 us (1%)
    pallas_call x1, Pallas kernels, per_device(): pl.pallas_call(functools.partial(kernel, nx, nd, ne), out_shape=jax.Shape...  90.9 us

profile of v3, /device:TPU:1, one launch (start us, length us, event | category | flops | bytes accessed | tf_op | source)
XLA Modules:
  0.0 92.3 jit_solution(9954350388559234093)
XLA Ops:
  0.0 90.9 %shard_map.91 = bf16[128,128]{1,0:T(8,128)(2,1)} custom-call(bf16[2048,128]{1,0:T(8,128)(2,1)} %strain_hbm.1, s32[16,128]{1,0:T(8,128)} %bitcast.3, s32[1,128]{1,0:T(1,128)} %bitcast.4, s32[1,128]{1,0:T(1,128)} %bitcast.5, bf16[128,4096]{1,0:T(8,128)(2,1)} %w1_hbm.1, bf16[4096,1024]{1,0:T(8,128)(2,1)} %w2_hbm.1, bf16[1024,128]{1,0:T(8,128)(2,1)} %outw_ref.1, ...), custom_call_target="tpu_custom_call" | custom-call | tf_op jit(solution)/shard_map/pallas_call | solution.py:391
  90.9 1.4 %copy.11 = bf16[128,128]{1,0:T(8,128)(2,1)} copy(bf16[128,128]{1,0:T(8,128)(2,1)} %shard_map.91) | data formatting | bytes 65536

commit v4 on v3

--- a/solution.py
+++ b/solution.py
@@ -57,6 +57,8 @@
     dispatch_v,
     combine_v,
     direct_v,
+    picks_v,
+    held_v,
     feats_v,
     x0_v,
     s0_v,
@@ -175,20 +177,28 @@
             ).start()
 
     def send_direct(src, dst, sem):
-        @pl.loop(1, nx * nd)
+        def send_to(to_d, offs):
+            for off in offs:
+                pltpu.make_async_remote_copy(
+                    src_ref=src.at[to_d * nx + off],
+                    dst_ref=dst.at[d * nx + (nx - off) % nx],
+                    send_sem=send_sem.at[sem],
+                    recv_sem=recv_sem.at[sem],
+                    device_id=(at_x(off), to_d),
+                    device_id_type=MESH,
+                ).start()
+
+        far_first = sorted(range(nx), key=lambda k: -min(k, nx - k))
+
+        @pl.loop(0, nd // 2)
         def _(i):
-            to = lax.rem(x * nd + d + i, nx * nd)
-            to_x, to_d = to // nd, to % nd
-            off = lax.rem(to_x - x + nx, nx)
-            pltpu.make_async_remote_copy(
-                src_ref=src.at[to_d * nx + off],
-                dst_ref=dst.at[d * nx + lax.rem(nx - off, nx)],
-                send_sem=send_sem.at[sem],
-                recv_sem=recv_sem.at[sem],
-                device_id=(to_x, to_d),
-                device_id_type=MESH,
-            ).start()
-
+            send_to(lax.rem(d + nd // 2 + i, nd), far_first)
+
+        @pl.loop(1, nd // 2)
+        def _(i):
+            send_to(lax.rem(d + i, nd), far_first)
+
+        send_to(d, [k for k in far_first if k])
         dst[pl.ds(d * nx, 1)] = src[pl.ds(d * nx, 1)]
         wait_bytes(dst.at[pl.ds(0, nx * nd - 1)], recv_sem.at[sem])
 
@@ -256,6 +266,15 @@
             device_id=(x, at_z(k)),
             device_id_type=MESH,
         ).start()
+    direct_v[...] = hot(
+        slot_code(at // 32, (at // 8) % 4 + (at // 2) % 4, at % 2).astype(F32)
+        == target_row
+    )
+    at = iota((n, rows), 1)
+    combine_v[...] = hot(
+        slot_code(at // 32, (at // 8) % 4 + (at // 2) % 4, at % 2).astype(F32)
+        == jnp.concatenate([spread(target_row)] * (rows // n), axis=1)
+    )
     z0_v[pl.ds(z, 1)] = s0_v[pl.ds(z, 1)]
     wait_bytes(z0_v.at[pl.ds(0, nz - 1)], recv_sem.at[1])
     for k in range(1, ne):
@@ -269,27 +288,12 @@
         ).start()
     a0_v[:, pl.ds(e, 1)] = z0_v[:, pl.ds(e, 1)]
     wait_bytes(a0_v.at[:, pl.ds(0, ne - 1)], recv_sem.at[5])
-    direct_v[...] = hot(
-        slot_code(at // 32, (at // 8) % 4 + (at // 2) % 4, at % 2).astype(F32)
-        == target_row
-    )
-    at = iota((n, rows), 1)
-    combine_v[...] = hot(
-        slot_code(at // 32, (at // 8) % 4 + (at // 2) % 4, at % 2).astype(F32)
-        == jnp.concatenate([spread(target_row)] * (rows // n), axis=1)
-    )
     pair_rows = nd * 16
-    forward(0)
-    forward(1)
     level = iota((pair_rows, n), 1)
     level_of = jnp.where(level < 48, level % 16, -1).astype(F32)
     for p in range(2):
         got = a0_v[:, :, 32 + 16 * p : 48 + 16 * p, :].reshape(pair_rows, n)
-        picks = hot(got.astype(F32) == level_of)
-        for c in range(CHUNKS):
-            cols = slice(c * ch, (c + 1) * ch)
-            scales_v[p, :, cols] = mm(picks, scale_v[:, cols])
-        forward(2 + p)
+        picks_v[p] = hot(got.astype(F32) == level_of)
 
     def widen(value, p):
         which = (iota((pair_rows, n), 0) // 2) % 2
@@ -304,16 +308,21 @@
         second_of = jnp.where(low_half, pltpu.roll(one, 4, axis=1), two)
         return first_of, second_of
 
-    def first(p, c):
+    def first(p, c, pick=False):
         cols = slice(c * ch, (c + 1) * ch)
         layer = w1_v[c, 2 * p : 2 * p + 2].reshape(2 * n, ch)
-        u = mm(xw_v[p], layer) * scales_v[p, :, cols]
+        if pick:
+            scales = mm(picks_v[p], scale_v[:, cols])
+            scales_v[p, :, cols] = scales
+        else:
+            scales = scales_v[p, :, cols]
+        u = mm(xw_v[p], layer) * scales
         h_v[p * pair_rows : (p + 1) * pair_rows, cols] = half_silu(u).astype(BF)
 
     def second(row, count, ranges, start, end):
-        @pl.loop(0, w2_v.shape[1] // 256)
+        @pl.loop(0, w2_v.shape[1] // 512)
         def _(t):
-            cols = pl.ds(pl.multiple_of(t * 256, 256), 256)
+            cols = pl.ds(pl.multiple_of(t * 512, 512), 512)
             part = None
             for lo, hi in ranges:
                 term = mm(h_v[row : row + count, lo:hi], w2_v[lo:hi, cols])
@@ -325,11 +334,11 @@
             else:
                 acc_v[0:count, cols] = part
 
-    def give_back(r_v, t_v, sem):
-        parts = []
-        for p in range(2):
-            total = mm(m_v[p * pair_rows : (p + 1) * pair_rows, :], outw_ref[...])
-            parts.append(total.reshape(rows // 16, 8, n))
+    def third(p):
+        total = mm(m_v[p * pair_rows : (p + 1) * pair_rows, :], outw_ref[...])
+        return total.reshape(rows // 16, 8, n)
+
+    def give_back(parts, r_v, t_v, sem):
         even, odd = swap(*parts)
         r_v[...] = jnp.stack([even, odd], axis=1).reshape(rows // 8, 8, n).astype(MSG)
         send_direct(r_v, t_v, sem)
@@ -339,23 +348,32 @@
         got = a0_v[:, :, 16 * p : 16 * p + 16, :]
         widen(got.reshape(pair_rows, n), p)
     w2_copy.wait()
-    for i in range(CHUNKS):
-        c = to_left[i]
-        own_copies[c].wait()
-        if i >= CHUNKS // 2:
-            w1_copies[1, c].wait_recv()
-            w1_copies[3, to_right[i]].wait_recv()
-        first(0, c)
     hid = w2_v.shape[0]
-    second(0, pair_rows, [(0, hid)], True, True)
-    for i in range(CHUNKS // 2):
-        ranges = []
-        for c in (to_right[i], to_left[i]):
+    for own in own_copies:
+        own.wait()
+
+    def span(chunks):
+        return [(c * ch, (c + 1) * ch) for c in chunks]
+
+    half = CHUNKS // 2
+    for i in range(half):
+        forward(i)
+        first(0, to_left[i], True)
+    second(0, pair_rows, [(hid // 2, hid)], True, False)
+    for i in range(half, CHUNKS):
+        w1_copies[1, to_left[i]].wait_recv()
+        first(0, to_left[i], True)
+    second(0, pair_rows, [(0, hid // 2)], False, True)
+    held_v[...] = third(0)
+    for i in range(half, CHUNKS):
+        w1_copies[3, to_right[i]].wait_recv()
+    for i in range(half):
+        chunks = to_right[i], to_left[i]
+        for c in chunks:
             w1_copies[2, c].wait_recv()
-            first(1, c)
-            ranges.append((c * ch, (c + 1) * ch))
-        second(pair_rows, pair_rows, ranges, i == 0, i == CHUNKS // 2 - 1)
-    values = give_back(r0_v, t0_v, 2)
+            first(1, c, True)
+        second(pair_rows, pair_rows, span(chunks), i == 0, i == half - 1)
+    values = give_back((held_v[...], third(1)), r0_v, t0_v, 2)
     features = (feats_v[...] + mm(values, back_ref[...])).astype(BF)
 
     q1_v[...] = mm(direct_v[...], features).reshape(rows // 8, 8, n).astype(MSG)
@@ -366,7 +384,7 @@
         for c in range(CHUNKS):
             first(p, c)
     second(0, rows, [(0, hid)], True, True)
-    out_ref[...] = give_back(r1_v, t1_v, 4)
+    out_ref[...] = give_back((third(0), third(1)), r1_v, t1_v, 4)
 
     for copy in w1_copies.values():
         copy.wait_send()
@@ -403,6 +421,8 @@
                 pltpu.VMEM((rows, nx * n), BF),
                 pltpu.VMEM((n, rows), BF),
                 pltpu.VMEM((rows, n), BF),
+                pltpu.VMEM((2, rows // 2, n), BF),
+                pltpu.VMEM((rows // 16, 8, n), F32),
                 pltpu.VMEM((n, n), F32),
                 pltpu.VMEM((nx, n + 16, n), BF),
                 pltpu.VMEM((nd // ne, ne, 64, n), BF),

time: 92.5 us -> 88.9 us (0.961)
  Pallas kernels: 90.9 us -> 87.3 us
    pallas_call x1, Pallas kernels: 90.9 us -> 87.3 us  [per_device(): pl.pallas_call(functools.partial(kernel, nx, nd, ne), out_shape=jax.Shape...]
where the time goes in v4:
time: 88.9 us; the launch traced here: 88.7 us
  Pallas kernels  87.3 us (98%)
  local copies, waits for them, and re-layouts  1.38 us (2%)
    pallas_call x1, Pallas kernels, per_device(): pl.pallas_call(functools.partial(kernel, nx, nd, ne), out_shape=jax.Shape...  87.3 us

profile of v4, /device:TPU:1, one launch (start us, length us, event | category | flops | bytes accessed | tf_op | source)
XLA Modules:
  0.0 88.7 jit_solution(7864678524980055120)
XLA Ops:
  0.0 87.3 %shard_map.91 = bf16[128,128]{1,0:T(8,128)(2,1)} custom-call(bf16[2048,128]{1,0:T(8,128)(2,1)} %strain_hbm.1, s32[16,128]{1,0:T(8,128)} %bitcast.3, s32[1,128]{1,0:T(1,128)} %bitcast.4, s32[1,128]{1,0:T(1,128)} %bitcast.5, bf16[128,4096]{1,0:T(8,128)(2,1)} %w1_hbm.1, bf16[4096,1024]{1,0:T(8,128)(2,1)} %w2_hbm.1, bf16[1024,128]{1,0:T(8,128)(2,1)} %outw_ref.1, ...), custom_call_target="tpu_custom_call" | custom-call | tf_op jit(solution)/shard_map/pallas_call | solution.py:409
  87.3 1.4 %copy.11 = bf16[128,128]{1,0:T(8,128)(2,1)} copy(bf16[128,128]{1,0:T(8,128)(2,1)} %shard_map.91) | data formatting | bytes 65536

commit v5 on v4

--- a/solution.py
+++ b/solution.py
@@ -39,15 +39,21 @@
     nd,
     ne,
     strain_hbm,
+    bands_hbm,
+    damaged_hbm,
+    owner_hbm,
+    w1_hbm,
+    w2_hbm,
+    outw_hbm,
+    scale_hbm,
+    back_hbm,
+    out_ref,
     bands_ref,
     damaged_ref,
     owner_ref,
-    w1_hbm,
-    w2_hbm,
     outw_ref,
     scale_ref,
     back_ref,
-    out_ref,
     strain_v,
     w1_v,
     w2_v,
@@ -108,6 +114,19 @@
     for k in range(1, ne):
         pl.semaphore_signal(barrier, inc=1, device_id=(x, at_e(k)), device_id_type=MESH)
 
+    small = []
+    for i, (src, dst) in enumerate(
+        (
+            (damaged_hbm, damaged_ref),
+            (bands_hbm, bands_ref),
+            (owner_hbm, owner_ref),
+            (scale_hbm, scale_ref),
+            (outw_hbm, outw_ref),
+            (back_hbm, back_ref),
+        )
+    ):
+        small.append(pltpu.make_async_copy(src, dst, local_sem.at[2 + i]))
+        small[i].start()
     strain_copy = pltpu.make_async_copy(strain_hbm, strain_v, local_sem.at[0])
     strain_copy.start()
     w2_copy = pltpu.make_async_copy(w2_hbm, w2_v, local_sem.at[1])
@@ -126,6 +145,8 @@
     def spread(row):
         return mm(jnp.where(eye, row, 0.0).astype(BF), ones)
 
+    for copy in small[:3]:
+        copy.wait()
     damaged = damaged_ref[...]
     high = spread((damaged // n).astype(F32))
     low = spread((damaged % n).astype(F32))
@@ -153,6 +174,8 @@
     feats_v[...] = feats
     x0_v[0, 0:n, :] = feats.astype(BF)
 
+    for copy in small[3:]:
+        copy.wait()
     half = scale_ref[...] * 0.5
     term0 = half.astype(BF)
     rest = half - term0.astype(F32)
@@ -320,9 +343,9 @@
         h_v[p * pair_rows : (p + 1) * pair_rows, cols] = half_silu(u).astype(BF)
 
     def second(row, count, ranges, start, end):
-        @pl.loop(0, w2_v.shape[1] // 512)
+        @pl.loop(0, w2_v.shape[1] // 1024)
         def _(t):
-            cols = pl.ds(pl.multiple_of(t * 512, 512), 512)
+            cols = pl.ds(pl.multiple_of(t * 1024, 1024), 1024)
             part = None
             for lo, hi in ranges:
                 term = mm(h_v[row : row + count, lo:hi], w2_v[lo:hi, cols])
@@ -409,9 +432,15 @@
         return pl.pallas_call(
             functools.partial(kernel, nx, nd, ne),
             out_shape=jax.ShapeDtypeStruct((n, outw.shape[1]), BF),
-            in_specs=[hbm, vmem, vmem, vmem, hbm, hbm, vmem, vmem, vmem],
+            in_specs=[hbm] * 9,
             out_specs=vmem,
             scratch_shapes=[
+                pltpu.VMEM((points // n, n), jnp.int32),
+                pltpu.VMEM((1, n), jnp.int32),
+                pltpu.VMEM((1, n), jnp.int32),
+                pltpu.VMEM(outw.shape, BF),
+                pltpu.VMEM(scale.shape, F32),
+                pltpu.VMEM(back.shape, BF),
                 pltpu.VMEM((points, n), BF),
                 pltpu.VMEM((CHUNKS, nx, n, hid // CHUNKS), BF),
                 pltpu.VMEM((hid, mid), BF),
@@ -438,7 +467,7 @@
                 pltpu.VMEM((rows // 8, 8, n), MSG),
                 pltpu.VMEM((rows // 8, 8, n), MSG),
                 pltpu.VMEM((rows // 8, 8, n), MSG),
-                pltpu.SemaphoreType.DMA((2,)),
+                pltpu.SemaphoreType.DMA((8,)),
                 pltpu.SemaphoreType.DMA((CHUNKS,)),
                 pltpu.SemaphoreType.DMA((3, CHUNKS)),
                 pltpu.SemaphoreType.DMA((nx, CHUNKS)),

time: 88.9 us -> 86.1 us (0.969)
  Pallas kernels: 87.3 us -> 84.5 us
    pallas_call x1, Pallas kernels: 87.3 us -> 84.5 us  [per_device(): pl.pallas_call(functools.partial(kernel, nx, nd, ne), out_shape=jax.Shape...]
where the time goes in v5:
time: 86.1 us; the launch traced here: 85.9 us
  Pallas kernels  84.5 us (98%)
  local copies, waits for them, and re-layouts  1.38 us (2%)
    pallas_call x1, Pallas kernels, per_device(): pl.pallas_call(functools.partial(kernel, nx, nd, ne), out_shape=jax.Shape...  84.5 us

profile of v5, /device:TPU:1, one launch (start us, length us, event | category | flops | bytes accessed | tf_op | source)
XLA Modules:
  0.0 85.9 jit_solution(9187443280129045754)
XLA Ops:
  0.0 84.5 %shard_map.91 = bf16[128,128]{1,0:T(8,128)(2,1)} custom-call(bf16[2048,128]{1,0:T(8,128)(2,1)} %strain_hbm.1, s32[16,128]{1,0:T(8,128)} %bitcast.3, s32[1,128]{1,0:T(1,128)} %bitcast.4, s32[1,128]{1,0:T(1,128)} %bitcast.5, bf16[128,4096]{1,0:T(8,128)(2,1)} %w1_hbm.1, bf16[4096,1024]{1,0:T(8,128)(2,1)} %w2_hbm.1, bf16[1024,128]{1,0:T(8,128)(2,1)} %outw_hbm.1, ...), custom_call_target="tpu_custom_call" | custom-call | tf_op jit(solution)/shard_map/pallas_call | solution.py:432
  84.5 1.4 %copy.11 = bf16[128,128]{1,0:T(8,128)(2,1)} copy(bf16[128,128]{1,0:T(8,128)(2,1)} %shard_map.91) | data formatting | bytes 65536
